TPU v7x, 512 devices: a whole 4x8x8 slice. The times are simulated.
512 devices in a mesh: rep: 16 (over y, z_hi), fsdp: 8 (over x, core), tp: 4 (over z_lo).
Axes of the slice: x: 4, y: 8, z: 8 (z_hi: 2, z_lo: 4; z = z_hi * 4 + z_lo), core: 2. Of those that a mesh axis runs over, the one named last changes fastest.
Arguments:
- tokens: bfloat16 [16, 2048, 4096], P('rep', 'fsdp', 'tp'), may hold values from -6 to 6
- key_weight: float32 [16, 4096, 1024], P('rep', 'fsdp', 'tp'), may hold values from -6 to 6
- value_weight: float32 [16, 4096, 1024], P('rep', 'fsdp', 'tp'), may hold values from -6 to 6
- key_momentum: float32 [16, 4096, 1024], P('rep', 'fsdp', 'tp'), may hold values from -4 to 4
- value_momentum: float32 [16, 4096, 1024], P('rep', 'fsdp', 'tp'), may hold values from -4 to 4
- key_cotangent: bfloat16 [16, 2048, 1024], P('rep', 'fsdp', 'tp'), may hold values from -6 to 6
- value_cotangent: bfloat16 [16, 2048, 1024], P('rep', 'fsdp', 'tp'), may hold values from -6 to 6
- step_number: int32 [1], replicated, may hold values from 0 to 999
Outputs:
- projected_keys: bfloat16 [16, 2048, 1024], P('rep', 'fsdp', 'tp')
- projected_values: bfloat16 [16, 2048, 1024], P('rep', 'fsdp', 'tp')
- averaged_key_weight: float32 [16, 4096, 1024], P('rep', 'fsdp', 'tp')
- averaged_value_weight: float32 [16, 4096, 1024], P('rep', 'fsdp', 'tp')
- key_velocity: float32 [16, 4096, 1024], P('rep', 'fsdp', 'tp')
- value_velocity: float32 [16, 4096, 1024], P('rep', 'fsdp', 'tp')
All inputs are finite; a program needn't handle non-finite values.
Results may differ from a plain program's by a relative error of at most 0.005.
Values may be sent and summed in bfloat16 or wider, within the bound.
No kernel may reach another device: no remote copies, remote signals or barrier semaphores. Data moves between devices by JAX's collectives and lax.ppermute only.
A program may use at most 64 MiB of HBM per device.

v0:
```python
from functools import partial

import jax
import jax.numpy as jnp
from jax import lax
from jax.sharding import PartitionSpec as P

D = 4096


momentum_decay = 0.9


def shortened(value):
    return jax.tree.map(lambda a: a.astype(jnp.bfloat16) if a.dtype == jnp.float32 else a, value)


def shifted(block, axis, distance):
    devices = range(lax.axis_size(axis))
    route = [((i - distance) % len(devices), i) for i in devices]
    return lax.ppermute(block, axis, route)


def partner_moved(params, distance):
    if distance == 0:
        return params
    return jax.tree.map(
        lambda part, own: part.astype(own.dtype),
        shifted(shortened(params), "rep", distance),
        params,
    )


def by_step(helper, params, selector):
    replicas = lax.axis_size("rep")
    branches = [partial(helper, distance=2**power % replicas) for power in range(4)]
    return lax.switch(selector, branches, params)


def body(
    tokens,
    key_weight,
    value_weight,
    key_momentum,
    value_momentum,
    key_cotangent,
    value_cotangent,
    step_number,
):
    scale = D ** (-0.5)
    inputs = tokens[0]
    width = key_weight.shape[2]
    selector = step_number[0] % 4
    learn = 0.5 * (step_number[0].astype(jnp.float32) + 1.0) / 1000.0
    master = jnp.concatenate([key_weight[0], value_weight[0]], axis=1)
    momentum = jnp.concatenate([key_momentum[0], value_momentum[0]], axis=1)
    whole = lax.all_gather(inputs, "tp", axis=1, tiled=True)
    block = lax.all_to_all(whole, "fsdp", split_axis=1, concat_axis=0, tiled=True)
    weight_bf = master.astype(jnp.bfloat16)
    projected = jnp.dot(
        whole,
        lax.all_gather(weight_bf, "fsdp", axis=0, tiled=True),
        preferred_element_type=jnp.float32,
    )
    projected = projected * scale
    keys_out = projected[:, :width].astype(jnp.bfloat16)
    values_out = projected[:, width:].astype(jnp.bfloat16)
    cotangent = jnp.concatenate([key_cotangent[0], value_cotangent[0]], axis=1)
    gradient = (
        lax.dot_general(
            block,
            lax.all_gather(cotangent, "fsdp", axis=0, tiled=True),
            (((0,), (0,)), ((), ())),
            preferred_element_type=jnp.float32,
        )
        * scale
    )
    velocity = momentum_decay * momentum + gradient
    moved = master - learn * velocity
    averaged = 0.5 * (moved + by_step(partner_moved, moved, selector))
    return (
        keys_out[None],
        values_out[None],
        averaged[:, :width][None],
        averaged[:, width:][None],
        velocity[:, :width][None],
        velocity[:, width:][None],
    )


def solution(mesh):
    placed = (
        P("rep", "fsdp", "tp"),
        P("rep", "fsdp", "tp"),
        P("rep", "fsdp", "tp"),
        P("rep", "fsdp", "tp"),
        P("rep", "fsdp", "tp"),
        P("rep", "fsdp", "tp"),
        P("rep", "fsdp", "tp"),
        P(),
    )
    return jax.shard_map(
        body,
        mesh=mesh,
        in_specs=placed,
        out_specs=(
            P("rep", "fsdp", "tp"),
            P("rep", "fsdp", "tp"),
            P("rep", "fsdp", "tp"),
            P("rep", "fsdp", "tp"),
            P("rep", "fsdp", "tp"),
            P("rep", "fsdp", "tp"),
        ),
        check_vma=False,
    )
```

profile of v0, /device:TPU:17, one launch (start us, length us, event | category | flops | bytes accessed | tf_op | source)
XLA Modules:
  0.0 163.0 jit_solution(10898675559461710627)
XLA Ops:
  7.2 2.1 %copy.46 = bf16[1,256,1024]{1,2,0:T(8,128)(2,1)} copy(bf16[1,256,1024]{2,1,0:T(8,128)(2,1)} %param.12) | data formatting | bytes 1048576 | tf_op args[0]
  9.4 1.7 %pad_maximum_fusion.1 = bf16[256,512]{1,0:T(8,128)(2,1)} fusion(bf16[256,256]{1,0:T(8,128)(2,1)} %bitcast.53, bf16[256,256]{1,0:T(8,128)(2,1)} %bitcast.54), kind=kLoop, calls=%fused_computation.17 | loop fusion | flops 524288 | bytes 524288 | tf_op jit(solution)/shard_map/concatenate | solution.py:68
  11.2 0.2 copy.45
  11.6 0.9 fusion.13
  12.5 55.9 %all-gather.9.cloned.1.call-done = bf16[1,256,4096]{1,2,0:T(8,128)(2,1)} async-done(((bf16[1,256,1024]{1,2,0:T(8,128)(2,1)}), bf16[1,256,4096]{1,2,0:T(8,128)(2,1)}) %all-gather.9.cloned.1.call-update) | async-done | bytes 2097168 | tf_op jit(solution)/shard_map/all_gather | solution.py:57
  68.4 5.2 %all-to-all-start = ((bf16[256,8,512]{0,2,1:T(8,128)(2,1)}), bf16[256,8,512]{0,2,1:T(8,128)(2,1)S(1)}, u32[]{:S(2)}, u32[]{:S(2)}) async-start(bf16[256,8,512]{0,2,1:T(8,128)(2,1)} %bitcast.52), calls=%async_computation | async-start | bytes 4194304 | tf_op jit(solution)/shard_map/all_to_all | solution.py:58
  74.2 2.0 %copy.48 = f32[1,512,256]{1,2,0:T(8,128)} copy(f32[1,512,256]{2,1,0:T(8,128)} %param.16) | data formatting | bytes 1048576 | tf_op args[4]
  76.3 2.0 %copy.47 = f32[1,512,256]{1,2,0:T(8,128)} copy(f32[1,512,256]{2,1,0:T(8,128)} %param.15) | data formatting | bytes 1048576 | tf_op args[3]
  78.3 30.0 %all-to-all-done = bf16[256,8,512]{0,2,1:T(8,128)(2,1)S(1)} async-done(((bf16[256,8,512]{0,2,1:T(8,128)(2,1)}), bf16[256,8,512]{0,2,1:T(8,128)(2,1)S(1)}, u32[]{:S(2)}, u32[]{:S(2)}) %all-to-all-start) | async-done | bytes 2097184 | tf_op jit(solution)/shard_map/all_to_all | solution.py:58
  108.3 2.5 %copy.49 = bf16[8,256,512]{2,1,0:T(8,128)(2,1)} copy(bf16[8,256,512]{1,2,0:T(8,128)(2,1)S(1)} %bitcast.44) | data formatting | bytes 4194304 | tf_op jit(solution)/shard_map/all_to_all | solution.py:58
  110.8 3.8 %multiply_subtract_fusion = (f32[512,512]{0,1:T(8,128)S(1)}, f32[512,512]{0,1:T(8,128)S(1)}) fusion(f32[512,256]{0,1:T(8,128)S(1)} %bitcast.47, f32[512,256]{0,1:T(8,128)S(1)} %bitcast.49, f32[]{:T(128)S(6)} %div.3, bf16[2048,512]{1,0:T(8,128)(2,1)} %all-gather.7.cloned.1.call-done, bf16[2048,512]{1,0:T(8,128)(2,1)} %bitcast.45, f32[512,256]{0,1:T(8,128)} %bitcast.50, ...), kind=kOutput, calls=%fused_computation.11 | convolution fusion | flops 1075576832 | bytes 8388612 | tf_op jit(solution)/shard_map/dot_general | solution.py:70
  114.6 32.5 %conditional.4 = (f32[512,512]{0,1:T(8,128)S(1)}) conditional(s32[]{:T(128)} %clamp.3, (f32[512,512]{0,1:T(8,128)S(1)}) %tuple.46, (f32[512,512]{0,1:T(8,128)S(1)}) %tuple.46, (f32[512,512]{0,1:T(8,128)S(1)}) %tuple.46, (f32[512,512]{0,1:T(8,128)S(1)}) %tuple.46), branch_computations={%region_0.1_spmd, %region_1.2_spmd, %region_2.3_spmd, %region_3.4_... | conditional | bytes 5242928
  114.6 0.2 copy.68
  114.8 5.3 %collective-permute-start.3 = (bf16[512,512]{1,0:T(8,128)(2,1)S(1)}, bf16[512,512]{1,0:T(8,128)(2,1)}, u32[]{:S(2)}, u32[]{:S(2)}) collective-permute-start(bf16[512,512]{1,0:T(8,128)(2,1)S(1)} %copy.68), channel_id=1, source_target_pairs={{256,0},{288,32},{320,64},{352,96},{384,128},{416,160},{448,192},{... | collective-permute-start | bytes 1572872 | tf_op jit(solution)/shard_map/cond/branch_3_fun/ppermute | solution.py:21
  120.1 25.6 %collective-permute-done.3 = bf16[512,512]{1,0:T(8,128)(2,1)} collective-permute-done((bf16[512,512]{1,0:T(8,128)(2,1)S(1)}, bf16[512,512]{1,0:T(8,128)(2,1)}, u32[]{:S(2)}, u32[]{:S(2)}) %collective-permute-start.3) | collective-permute-done | bytes 524320 | tf_op jit(solution)/shard_map/cond/branch_3_fun/ppermute | solution.py:21
  145.8 1.3 copy.64
  147.1 0.2 add_multiply_fusion
  147.4 1.0 copy.57
  148.4 1.0 copy.58
  149.4 1.0 copy.59
  150.4 1.0 copy.60
  151.4 3.4 %fusion.10 = bf16[256,512]{0,1:T(8,128)(2,1)S(1)} fusion(bf16[4096,512]{0,1:T(8,128)(2,1)} %all-gather.5.cloned.1.call-done, bf16[1,256,4096]{1,2,0:T(8,128)(2,1)S(1)} %copy-done), kind=kOutput, calls=%fused_computation.7 | convolution fusion | flops 1074003968 | bytes 6553600 | tf_op jit(solution)/shard_map/dot_general | solution.py:60
  154.9 0.8 copy.55
  155.7 0.8 copy.56
  (18 shorter events, 0.5 us)
Async XLA Ops:
  7.2 4.0 %copy-start.1 = (f32[1,512,256]{2,1,0:T(8,128)S(1)}, f32[1,512,256]{2,1,0:T(8,128)}, u32[]{:S(2)}) copy-start(f32[1,512,256]{2,1,0:T(8,128)} %param.14) | copy-start | bytes 1572868
  7.2 4.2 %copy-start.2 = (f32[1,512,256]{2,1,0:T(8,128)S(1)}, f32[1,512,256]{2,1,0:T(8,128)}, u32[]{:S(2)}) copy-start(f32[1,512,256]{2,1,0:T(8,128)} %param.13) | copy-start | bytes 1572868
  7.2 61.2 %all-gather.9.cloned.1.call-start = ((), (), s32[]{:S(2)}) async-start(), calls=%async_computation.3 | async-start | bytes 2621440 | tf_op jit(solution)/shard_map/all_gather | solution.py:57
  9.4 101.4 %all-gather.7.cloned.1.call-start = ((), (), s32[]{:S(2)}) async-start(), calls=%async_computation.2 | async-start | bytes 2359296 | tf_op jit(solution)/shard_map/all_gather | solution.py:72
  11.1 140.3 %all-gather.5.cloned.1.call-start = ((), (), s32[]{:S(2)}) async-start(), calls=%async_computation.1 | async-start | bytes 4718592 | tf_op jit(solution)/shard_map/all_gather | solution.py:62
  68.4 39.9 %all-to-all-start = ((bf16[256,8,512]{0,2,1:T(8,128)(2,1)}), bf16[256,8,512]{0,2,1:T(8,128)(2,1)S(1)}, u32[]{:S(2)}, u32[]{:S(2)}) async-start(bf16[256,8,512]{0,2,1:T(8,128)(2,1)} %bitcast.52), calls=%async_computation | async-start | bytes 4194304 | tf_op jit(solution)/shard_map/all_to_all | solution.py:58
  114.8 30.9 %collective-permute-start.3 = (bf16[512,512]{1,0:T(8,128)(2,1)S(1)}, bf16[512,512]{1,0:T(8,128)(2,1)}, u32[]{:S(2)}, u32[]{:S(2)}) collective-permute-start(bf16[512,512]{1,0:T(8,128)(2,1)S(1)} %copy.68), channel_id=1, source_target_pairs={{256,0},{288,32},{320,64},{352,96},{384,128},{416,160},{448,192},{... | collective-permute-start | bytes 1572872 | tf_op jit(solution)/shard_map/cond/branch_3_fun/ppermute | solution.py:21
  149.4 2.0 %copy-start = (bf16[1,256,4096]{1,2,0:T(8,128)(2,1)S(1)}, bf16[1,256,4096]{1,2,0:T(8,128)(2,1)}, u32[]{:S(2)}) copy-start(bf16[1,256,4096]{1,2,0:T(8,128)(2,1)} %all-gather.9.cloned.1.call-done) | copy-start | bytes 6291460
Sparse Core Ops, SparseCore 0:
  10.7 57.6 all-gather.8
  71.1 36.8 all-gather.6
  110.2 37.2 all-gather.4
where the time goes:
time: 163 us
  waiting for transfers between devices  112 us (69%)
  local copies, waits for them, and re-layouts  16.2 us (10%)
  between operations  14.5 us (9%)
  starting transfers between devices  10.6 us (7%)
  matrix products  7.21 us (4%)
  other arithmetic  2.78 us (2%)
    all_gather x1, waiting for transfers between devices, body(): whole = lax.all_gather(inputs, 'tp', axis=1, tiled=True)  55.9 us
    all_to_all x1, waiting for transfers between devices, body(): lax.all_to_all(whole, 'fsdp', split_axis=1, concat_axis=0, tiled=True)  30 us
    ppermute x1, waiting for transfers between devices, shifted(): return lax.ppermute(block, axis, route)  25.6 us
    unnamed x17, local copies, waits for them, and re-layouts  12.1 us
    ppermute x1, starting transfers between devices, shifted(): return lax.ppermute(block, axis, route)  5.29 us
    all_to_all x1, starting transfers between devices, body(): lax.all_to_all(whole, 'fsdp', split_axis=1, concat_axis=0, tiled=True)  5.18 us
    dot_general x1, matrix products, body(): lax.dot_general(block, lax.all_gather(cotangent, 'fsdp', axis=0, tiled=Tr...  3.77 us
    dot_general x1, matrix products, body(): jnp.dot(whole, lax.all_gather(weight_bf, 'fsdp', axis=0, tiled=True), pre...  3.43 us
  transfers between devices with their start and end apart: 5, of which 3 were waited for; matrix products, arithmetic and copies ran while one was open for 12% of the time, Pallas kernels for 0%

commit v1 on v0

v1 whole, which is shorter than its diff:
```python
from functools import partial

import jax
import jax.numpy as jnp
from jax import lax
from jax.experimental import pallas as pl
from jax.experimental.pallas import tpu as pltpu
from jax.sharding import PartitionSpec as P

D = 4096
scale = D ** (-0.5)
momentum_decay = 0.9
chunks = 2
bf16 = jnp.bfloat16
f32 = jnp.float32

vmem = pl.BlockSpec(memory_space=pltpu.VMEM)
smem = pl.BlockSpec(memory_space=pltpu.SMEM)


def call(kernel, outs, *operands, scratch=(), scalars=0, aliases=None, flops=0):
    moved = sum(a.size * a.dtype.itemsize for a in operands)
    moved += sum(o.size * o.dtype.itemsize for o in outs)
    return pl.pallas_call(
        kernel,
        out_shape=outs,
        in_specs=[smem] * scalars + [vmem] * (len(operands) - scalars),
        out_specs=[vmem] * len(outs),
        scratch_shapes=list(scratch),
        input_output_aliases=aliases or {},
        compiler_params=pltpu.CompilerParams(vmem_limit_bytes=24 * 2**20),
        cost_estimate=pl.CostEstimate(flops=flops, bytes_accessed=moved, transcendentals=0),
    )(*operands)


def like(shape, dtype):
    return jax.ShapeDtypeStruct(shape, dtype)


def across(block):
    return lax.ppermute(block, "fsdp", [(i, i ^ 1) for i in range(lax.axis_size("fsdp"))])


def around(block, hops):
    count = lax.axis_size("fsdp")
    return lax.ppermute(block, "fsdp", [(i, (i + 2 * hops) % count) for i in range(count)])


def swapped(block, mask):
    return lax.ppermute(block, "tp", [(i, i ^ mask) for i in range(lax.axis_size("tp"))])


def from_partner(block, distance):
    count = lax.axis_size("rep")
    return lax.ppermute(block, "rep", [(i, (i + distance) % count) for i in range(count)])


def split_kernel(core_ref, tokens_ref, own_ref, other_ref):
    half = own_ref.shape[1]
    core = core_ref[0]
    own_ref[...] = tokens_ref[0, :, pl.ds(pl.multiple_of(core * half, half), half)]
    other_ref[...] = tokens_ref[0, :, pl.ds(pl.multiple_of((1 - core) * half, half), half)]


def join_kernel(own_ref, other_ref, *part_refs):
    rows = own_ref.shape[0]
    for at, part in enumerate(part_refs):
        width = part.shape[1]
        part[:rows] = own_ref[:, at * width : (at + 1) * width]
        part[rows:] = other_ref[:, at * width : (at + 1) * width]


def beside_kernel(key_ref, value_ref, out_ref):
    width = key_ref.shape[2]
    out_ref[:, :width] = key_ref[0].astype(bf16)
    out_ref[:, width:] = value_ref[0].astype(bf16)


def partial_kernel(at_ref, a0, a1, a2, a3, cot_own, cot_other, p0, p1, p2, p3, held):
    tokens = cot_own.shape[0]
    for j, a in enumerate((a0, a1, a2, a3)):
        held[j] = a[...]
    for k, p in enumerate((p0, p1, p2, p3)):
        j = at_ref[k]
        total = lax.dot_general(
            held[j, :tokens], cot_own[...], (((0,), (0,)), ((), ())), preferred_element_type=f32
        )
        total += lax.dot_general(
            held[j, tokens:], cot_other[...], (((0,), (0,)), ((), ())), preferred_element_type=f32
        )
        p[...] = (total * scale).astype(p.dtype)


def update_kernel(
    at, learn_ref, p0, r1, r2, r3, kw, vw, km, vm, velocity_ref, moved_ref, short_ref
):
    rows = p0.shape[0]
    width = kw.shape[2]
    part = pl.ds(at * rows, rows)
    learn = learn_ref[0]
    gradient = p0[...] + r1[...].astype(f32) + r2[...].astype(f32) + r3[...].astype(f32)
    for i, (w, m) in enumerate(((kw, km), (vw, vm))):
        cols = slice(i * width, (i + 1) * width)
        velocity = momentum_decay * m[0, part] + gradient[:, cols]
        moved = w[0, part] - learn * velocity
        velocity_ref[:, cols] = velocity
        moved_ref[:, cols] = moved
        short_ref[:, cols] = moved.astype(bf16)


def finish_kernel(*refs):
    outs = refs[-4:]
    width = outs[0].shape[2]
    for at in range(chunks):
        velocity, moved, other = refs[3 * at : 3 * at + 3]
        rows = velocity.shape[0]
        part = pl.ds(at * rows, rows)
        averaged = 0.5 * (moved[...] + other[...].astype(f32))
        outs[0][0, part] = averaged[:, :width]
        outs[1][0, part] = averaged[:, width:]
        outs[2][0, part] = velocity[:, :width]
        outs[3][0, part] = velocity[:, width:]


def project_kernel(at_ref, *refs):
    acts, weights = refs[: 4 * chunks], refs[4 * chunks : 4 * chunks + 4]
    mine_ref, other_ref, held = refs[4 * chunks + 4 :]
    for i, a in enumerate(acts):
        held[i] = a[...]
    depth = held.shape[2]
    total = None
    for k, w in enumerate(weights):
        for at in range(chunks):
            term = jnp.dot(
                held[4 * at + at_ref[k]],
                w[at * depth : (at + 1) * depth],
                preferred_element_type=f32,
            )
            total = term if total is None else total + term
    rows = mine_ref.shape[0]
    mine_ref[...] = total[:rows]
    other_ref[...] = total[rows:].astype(bf16)


def project_end_kernel(mine_ref, other_ref, key_ref, value_ref):
    width = key_ref.shape[2]
    total = (mine_ref[...] + other_ref[...].astype(f32)) * scale
    key_ref[0] = total[:, :width].astype(bf16)
    value_ref[0] = total[:, width:].astype(bf16)


def step(tokens, kw, vw, km, vm, kc, vc, learn, core, order, distance):
    _, rows, features = tokens.shape
    _, depth, width = kw.shape
    half = features // 2
    both = 2 * width
    own, other = call(
        split_kernel, [like((rows, half), bf16)] * 2, core, tokens, scalars=1
    )
    arrived = across(other)
    cot_own = call(beside_kernel, [like((rows, both), bf16)], kc, vc)[0]
    weight = call(beside_kernel, [like((depth, both), bf16)], kw, vw)[0]
    parts = call(
        join_kernel, [like((2 * rows, half // chunks), bf16)] * chunks, own, arrived
    )
    cot_other = across(cot_own)
    weights = (weight, around(weight, -1), around(weight, 2), around(weight, 1))
    piece = depth // chunks
    kept, acts = [], []
    for at, a0 in enumerate(parts):
        a3 = swapped(a0, 3)
        a1 = swapped(a0, 1)
        a2 = swapped(a3, 1)
        acts += [a0, a1, a2, a3]
        p0, p1, p2, p3 = call(
            partial_kernel,
            [like((piece, both), f32)] + [like((piece, both), bf16)] * 3,
            order, a0, a1, a2, a3, cot_own, cot_other,
            scalars=1,
            scratch=[pltpu.VMEM((4,) + a0.shape, bf16)],
            flops=2 * 4 * piece * both * 2 * rows,
        )
        r1, r2, r3 = around(p1, 1), around(p2, 2), around(p3, -1)
        velocity, moved, short = call(
            partial(update_kernel, at),
            [like((piece, both), f32)] * 2 + [like((piece, both), bf16)],
            learn, p0, r1, r2, r3, kw, vw, km, vm,
            scalars=1,
        )
        kept += [velocity, moved, from_partner(short, distance)]
    mine, sent = call(
        project_kernel,
        [like((rows, both), f32), like((rows, both), bf16)],
        order, *acts, *weights,
        scalars=1,
        scratch=[pltpu.VMEM((4 * chunks,) + acts[0].shape, bf16)],
        flops=2 * 2 * rows * both * 4 * depth,
    )
    keys_out, values_out = call(
        project_end_kernel, [like((1, rows, width), bf16)] * 2, mine, across(sent)
    )
    averaged_key, averaged_value, key_velocity, value_velocity = call(
        finish_kernel, [like((1, depth, width), f32)] * 4, *kept
    )
    return keys_out, values_out, averaged_key, averaged_value, key_velocity, value_velocity


def body(tokens, kw, vw, km, vm, kc, vc, step_number):
    replicas = lax.axis_size("rep")
    at_x, core = lax.axis_index("fsdp") // 2, lax.axis_index("fsdp") % 2
    at_z = lax.axis_index("tp")
    order = jnp.stack([jnp.bitwise_xor((at_x + k) % 4, at_z) for k in range(4)]).astype(jnp.int32)
    learn = 0.5 * (step_number.astype(f32) + 1.0) / 1000.0
    branches = [partial(step, distance=2**power % replicas) for power in range(4)]
    return lax.switch(
        step_number[0] % 4,
        branches,
        tokens, kw, vw, km, vm, kc, vc, learn, core.reshape(1).astype(jnp.int32), order,
    )


def solution(mesh):
    spread = P("rep", "fsdp", "tp")
    return jax.shard_map(
        body,
        mesh=mesh,
        in_specs=(spread,) * 7 + (P(),),
        out_specs=(spread,) * 6,
        check_vma=False,
    )
```

time: 163 us -> 105 us (0.64)
  the two profiles are of different devices: /device:TPU:17 before, /device:TPU:33 now
where the time goes in v1:
time: 105 us; the launch traced here: 104 us
  starting transfers between devices  65.2 us (62%)
  waiting for transfers between devices  28.3 us (27%)
  Pallas kernels  8.42 us (8%)
  between operations  1.43 us (1%)
    ppermute x9, starting transfers between devices, around(): lax.ppermute(block, 'fsdp', [(i, (i + 2 * hops) % count) for i in range(c...  28.8 us
    ppermute x6, starting transfers between devices, swapped(): lax.ppermute(block, 'tp', [(i, i ^ mask) for i in range(lax.axis_size('tp...  21.7 us
    ppermute x2, waiting for transfers between devices, from_partner(): lax.ppermute(block, 'rep', [(i, (i + distance) % count) for i in range(co...  20.7 us
    ppermute x3, starting transfers between devices, across(): lax.ppermute(block, 'fsdp', [(i, i ^ 1) for i in range(lax.axis_size('fsd...  9.83 us
    pallas_call x11, Pallas kernels, call(): pl.pallas_call(kernel, out_shape=outs, in_specs=[smem] * scalars + [vmem]...  8.42 us
    ppermute x9, waiting for transfers between devices, around(): lax.ppermute(block, 'fsdp', [(i, (i + 2 * hops) % count) for i in range(c...  5.33 us
    ppermute x2, starting transfers between devices, from_partner(): lax.ppermute(block, 'rep', [(i, (i + distance) % count) for i in range(co...  4.84 us
  transfers between devices with their start and end apart: 20, of which 8 were waited for; matrix products, arithmetic and copies ran while one was open for 0% of the time, Pallas kernels for 6%

profile of v1, /device:TPU:33, one launch (start us, length us, event | category | flops | bytes accessed | tf_op | source)
XLA Modules:
  0.0 103.9 jit_solution(4404243395502273103)
XLA Ops:
  1.6 102.3 %conditional.1 = (bf16[1,256,256]{2,1,0:T(8,128)(2,1)}, bf16[1,256,256]{2,1,0:T(8,128)(2,1)}, f32[1,512,256]{2,1,0:T(8,128)}, f32[1,512,256]{2,1,0:T(8,128)}, f3...) conditional(s32[]{:T(128)} %clamp.3, (s32[1]{0:T(128)}, ...), branch_computations={%region_0.1_spmd, %region_1.2_spmd, %region_2.3_spmd, %region_3.4_... | conditional | flops 2147483648 | bytes 63177752 | solution.py:215
  2.7 2.6 %collective-permute-start.40 = (bf16[256,512]{1,0:T(8,128)(2,1)S(1)}, bf16[256,512]{1,0:T(8,128)(2,1)S(1)}, u32[]{:S(2)}, u32[]{:S(2)}) collective-permute-start(bf16[256,512]{1,0:T(8,128)(2,1)S(1)} %get-tuple-element.156), channel_id=1, source_target_pairs={{0,4},{4,0},{8,12},{12,8},{16,20},{20,16},{24,28},{28,24},{1,5},{5... | collective-permute-start | bytes 786440 | tf_op jit(solution)/shard_map/cond/branch_2_fun/ppermute | solution.py:41
  6.4 7.7 %collective-permute-start.42 = (bf16[512,256]{1,0:T(8,128)(2,1)S(1)}, bf16[512,256]{1,0:T(8,128)(2,1)S(1)}, u32[]{:S(2)}, u32[]{:S(2)}) collective-permute-start(bf16[512,256]{1,0:T(8,128)(2,1)S(1)} %get-tuple-element.157.refs_0_.a0), channel_id=1, source_target_pairs={{0,3},{1,2},{2,1},{3,0},{4,7},{5,6},{6,5},{7,4},{8,11},{9,10},{10,... | collective-permute-start | bytes 786440 | tf_op jit(solution)/shard_map/cond/branch_2_fun/ppermute | solution.py:50
  14.2 2.6 %collective-permute-start.51 = (bf16[256,512]{1,0:T(8,128)(2,1)S(1)}, bf16[256,512]{1,0:T(8,128)(2,1)S(1)}, u32[]{:S(2)}, u32[]{:S(2)}) collective-permute-start(bf16[256,512]{1,0:T(8,128)(2,1)S(1)} %branch_2_fun.16.cot_own), channel_id=1, source_target_pairs={{0,4},{4,0},{8,12},{12,8},{16,20},{20,16},{24,28},{28,24},{1,5},{5... | collective-permute-start | bytes 786440 | tf_op jit(solution)/shard_map/cond/branch_2_fun/ppermute | solution.py:41
  16.8 1.9 %collective-permute-start.41 = (bf16[512,256]{1,0:T(8,128)(2,1)S(1)}, bf16[512,256]{1,0:T(8,128)(2,1)S(1)}, u32[]{:S(2)}, u32[]{:S(2)}) collective-permute-start(bf16[512,256]{1,0:T(8,128)(2,1)S(1)} %get-tuple-element.157.refs_0_.a0), channel_id=1, source_target_pairs={{0,1},{1,0},{2,3},{3,2},{4,5},{5,4},{6,7},{7,6},{8,9},{9,8},{10,11... | collective-permute-start | bytes 786440 | tf_op jit(solution)/shard_map/cond/branch_2_fun/ppermute | solution.py:50
  18.7 1.9 %collective-permute-start.45 = (bf16[512,256]{1,0:T(8,128)(2,1)S(1)}, bf16[512,256]{1,0:T(8,128)(2,1)S(1)}, u32[]{:S(2)}, u32[]{:S(2)}) collective-permute-start(bf16[512,256]{1,0:T(8,128)(2,1)S(1)} %get-tuple-element.158.refs_4_.a0), channel_id=1, source_target_pairs={{0,3},{1,2},{2,1},{3,0},{4,7},{5,6},{6,5},{7,4},{8,11},{9,10},{10,... | collective-permute-start | bytes 786440 | tf_op jit(solution)/shard_map/cond/branch_2_fun/ppermute | solution.py:50
  20.7 4.4 %collective-permute-start.47 = (bf16[512,512]{1,0:T(8,128)(2,1)S(1)}, bf16[512,512]{1,0:T(8,128)(2,1)S(1)}, u32[]{:S(2)}, u32[]{:S(2)}) collective-permute-start(bf16[512,512]{1,0:T(8,128)(2,1)S(1)} %branch_2_fun.13.refs_8_), channel_id=1, source_target_pairs={{0,24},{4,28},{8,0},{12,4},{16,8},{20,12},{24,16},{28,20},{1,25},{... | collective-permute-start | bytes 1572872 | tf_op jit(solution)/shard_map/cond/branch_2_fun/ppermute | solution.py:46
  25.2 3.4 %collective-permute-start.43 = (bf16[512,256]{1,0:T(8,128)(2,1)S(1)}, bf16[512,256]{1,0:T(8,128)(2,1)S(1)}, u32[]{:S(2)}, u32[]{:S(2)}) collective-permute-start(bf16[512,256]{1,0:T(8,128)(2,1)S(1)} %collective-permute-done.42.refs_3_.a3), channel_id=1, source_target_pairs={{0,1},{1,0},{2,3},{3,2},{4,5},{5,4},{6,7},{7,6},{8,9},{9,8},{10,11... | collective-permute-start | bytes 786440 | tf_op jit(solution)/shard_map/cond/branch_2_fun/ppermute | solution.py:50
  28.5 2.7 %collective-permute-start.48 = (bf16[512,512]{1,0:T(8,128)(2,1)S(1)}, bf16[512,512]{1,0:T(8,128)(2,1)S(1)}, u32[]{:S(2)}, u32[]{:S(2)}) collective-permute-start(bf16[512,512]{1,0:T(8,128)(2,1)S(1)} %branch_2_fun.13.refs_8_), channel_id=1, source_target_pairs={{0,16},{4,20},{8,24},{12,28},{16,0},{20,4},{24,8},{28,12},{1,17},{... | collective-permute-start | bytes 1572872 | tf_op jit(solution)/shard_map/cond/branch_2_fun/ppermute | solution.py:46
  31.2 2.3 %collective-permute-start.49 = (bf16[512,512]{1,0:T(8,128)(2,1)S(1)}, bf16[512,512]{1,0:T(8,128)(2,1)S(1)}, u32[]{:S(2)}, u32[]{:S(2)}) collective-permute-start(bf16[512,512]{1,0:T(8,128)(2,1)S(1)} %branch_2_fun.13.refs_8_), channel_id=1, source_target_pairs={{0,8},{4,12},{8,16},{12,20},{16,24},{20,28},{24,0},{28,4},{1,9},{5... | collective-permute-start | bytes 1572872 | tf_op jit(solution)/shard_map/cond/branch_2_fun/ppermute | solution.py:46
  33.5 4.4 %collective-permute-start.44 = (bf16[512,256]{1,0:T(8,128)(2,1)S(1)}, bf16[512,256]{1,0:T(8,128)(2,1)S(1)}, u32[]{:S(2)}, u32[]{:S(2)}) collective-permute-start(bf16[512,256]{1,0:T(8,128)(2,1)S(1)} %get-tuple-element.158.refs_4_.a0), channel_id=1, source_target_pairs={{0,1},{1,0},{2,3},{3,2},{4,5},{5,4},{6,7},{7,6},{8,9},{9,8},{10,11... | collective-permute-start | bytes 786440 | tf_op jit(solution)/shard_map/cond/branch_2_fun/ppermute | solution.py:50
  38.2 2.4 %collective-permute-start.46 = (bf16[512,256]{1,0:T(8,128)(2,1)S(1)}, bf16[512,256]{1,0:T(8,128)(2,1)S(1)}, u32[]{:S(2)}, u32[]{:S(2)}) collective-permute-start(bf16[512,256]{1,0:T(8,128)(2,1)S(1)} %collective-permute-done.45.refs_7_.a3), channel_id=1, source_target_pairs={{0,1},{1,0},{2,3},{3,2},{4,5},{5,4},{6,7},{7,6},{8,9},{9,8},{10,11... | collective-permute-start | bytes 786440 | tf_op jit(solution)/shard_map/cond/branch_2_fun/ppermute | solution.py:50
  42.8 3.3 %collective-permute-start.52 = (bf16[256,512]{1,0:T(8,128)(2,1)S(1)}, bf16[256,512]{1,0:T(8,128)(2,1)S(1)}, u32[]{:S(2)}, u32[]{:S(2)}) collective-permute-start(bf16[256,512]{1,0:T(8,128)(2,1)S(1)} %get-tuple-element.169), channel_id=1, source_target_pairs={{0,8},{4,12},{8,16},{12,20},{16,24},{20,28},{24,0},{28,4},{1,9},{5... | collective-permute-start | bytes 786440 | tf_op jit(solution)/shard_map/cond/branch_2_fun/ppermute | solution.py:46
  47.4 3.4 %collective-permute-start.53 = (bf16[256,512]{1,0:T(8,128)(2,1)S(1)}, bf16[256,512]{1,0:T(8,128)(2,1)S(1)}, u32[]{:S(2)}, u32[]{:S(2)}) collective-permute-start(bf16[256,512]{1,0:T(8,128)(2,1)S(1)} %get-tuple-element.170), channel_id=1, source_target_pairs={{0,16},{4,20},{8,24},{12,28},{16,0},{20,4},{24,8},{28,12},{1,17},{... | collective-permute-start | bytes 786440 | tf_op jit(solution)/shard_map/cond/branch_2_fun/ppermute | solution.py:46
  50.8 4.0 %collective-permute-start.54 = (bf16[256,512]{1,0:T(8,128)(2,1)S(1)}, bf16[256,512]{1,0:T(8,128)(2,1)S(1)}, u32[]{:S(2)}, u32[]{:S(2)}) collective-permute-start(bf16[256,512]{1,0:T(8,128)(2,1)S(1)} %get-tuple-element.171), channel_id=1, source_target_pairs={{0,24},{4,28},{8,0},{12,4},{16,8},{20,12},{24,16},{28,20},{1,25},{... | collective-permute-start | bytes 786440 | tf_op jit(solution)/shard_map/cond/branch_2_fun/ppermute | solution.py:46
  56.1 2.5 %collective-permute-start.56 = (bf16[256,512]{1,0:T(8,128)(2,1)S(1)}, bf16[256,512]{1,0:T(8,128)(2,1)S(1)}, u32[]{:S(2)}, u32[]{:S(2)}) collective-permute-start(bf16[256,512]{1,0:T(8,128)(2,1)S(1)} %get-tuple-element.178), channel_id=1, source_target_pairs={{0,8},{4,12},{8,16},{12,20},{16,24},{20,28},{24,0},{28,4},{1,9},{5... | collective-permute-start | bytes 786440 | tf_op jit(solution)/shard_map/cond/branch_2_fun/ppermute | solution.py:46
  58.7 3.7 %collective-permute-start.57 = (bf16[256,512]{1,0:T(8,128)(2,1)S(1)}, bf16[256,512]{1,0:T(8,128)(2,1)S(1)}, u32[]{:S(2)}, u32[]{:S(2)}) collective-permute-start(bf16[256,512]{1,0:T(8,128)(2,1)S(1)} %get-tuple-element.179), channel_id=1, source_target_pairs={{0,16},{4,20},{8,24},{12,28},{16,0},{20,4},{24,8},{28,12},{1,17},{... | collective-permute-start | bytes 786440 | tf_op jit(solution)/shard_map/cond/branch_2_fun/ppermute | solution.py:46
  63.8 2.6 %collective-permute-start.58 = (bf16[256,512]{1,0:T(8,128)(2,1)S(1)}, bf16[256,512]{1,0:T(8,128)(2,1)S(1)}, u32[]{:S(2)}, u32[]{:S(2)}) collective-permute-start(bf16[256,512]{1,0:T(8,128)(2,1)S(1)} %get-tuple-element.180), channel_id=1, source_target_pairs={{0,24},{4,28},{8,0},{12,4},{16,8},{20,12},{24,16},{28,20},{1,25},{... | collective-permute-start | bytes 786440 | tf_op jit(solution)/shard_map/cond/branch_2_fun/ppermute | solution.py:46
  68.4 4.7 %collective-permute-start.50 = (bf16[256,512]{1,0:T(8,128)(2,1)S(1)}, bf16[256,512]{1,0:T(8,128)(2,1)S(1)}, u32[]{:S(2)}, u32[]{:S(2)}) collective-permute-start(bf16[256,512]{1,0:T(8,128)(2,1)S(1)} %get-tuple-element.162), channel_id=1, source_target_pairs={{0,4},{4,0},{8,12},{12,8},{16,20},{20,16},{24,28},{28,24},{1,5},{5... | collective-permute-start | bytes 786440 | tf_op jit(solution)/shard_map/cond/branch_2_fun/ppermute | solution.py:41
  73.4 2.4 %collective-permute-start.55 = (bf16[256,512]{1,0:T(8,128)(2,1)S(1)}, bf16[256,512]{1,0:T(8,128)(2,1)S(1)}, u32[]{:S(2)}, u32[]{:S(2)}) collective-permute-start(bf16[256,512]{1,0:T(8,128)(2,1)S(1)} %get-tuple-element.176), channel_id=1, source_target_pairs={{0,128},{32,160},{64,192},{96,224},{128,256},{160,288},{192,320},{... | collective-permute-start | bytes 786440 | tf_op jit(solution)/shard_map/cond/branch_2_fun/ppermute | solution.py:55
  75.8 2.5 %collective-permute-done.57.r2 = bf16[256,512]{1,0:T(8,128)(2,1)S(1)} collective-permute-done((bf16[256,512]{1,0:T(8,128)(2,1)S(1)}, bf16[256,512]{1,0:T(8,128)(2,1)S(1)}, u32[]{:S(2)}, u32[]{:S(2)}) %collective-permute-start.57) | collective-permute-done | bytes 262176 | tf_op jit(solution)/shard_map/cond/branch_2_fun/ppermute | solution.py:46
  78.5 2.4 %collective-permute-start.59 = (bf16[256,512]{1,0:T(8,128)(2,1)S(1)}, bf16[256,512]{1,0:T(8,128)(2,1)S(1)}, u32[]{:S(2)}, u32[]{:S(2)}) collective-permute-start(bf16[256,512]{1,0:T(8,128)(2,1)S(1)} %get-tuple-element.183), channel_id=1, source_target_pairs={{0,128},{32,160},{64,192},{96,224},{128,256},{160,288},{192,320},{... | collective-permute-start | bytes 786440 | tf_op jit(solution)/shard_map/cond/branch_2_fun/ppermute | solution.py:55
  81.7 7.6 %collective-permute-done.55.refs_2_ = bf16[256,512]{1,0:T(8,128)(2,1)S(1)} collective-permute-done((bf16[256,512]{1,0:T(8,128)(2,1)S(1)}, bf16[256,512]{1,0:T(8,128)(2,1)S(1)}, u32[]{:S(2)}, u32[]{:S(2)}) %collective-permute-start.55) | collective-permute-done | bytes 262176 | tf_op jit(solution)/shard_map/cond/branch_2_fun/ppermute | solution.py:55
  89.3 13.1 %collective-permute-done.59.refs_5_ = bf16[256,512]{1,0:T(8,128)(2,1)S(1)} collective-permute-done((bf16[256,512]{1,0:T(8,128)(2,1)S(1)}, bf16[256,512]{1,0:T(8,128)(2,1)S(1)}, u32[]{:S(2)}, u32[]{:S(2)}) %collective-permute-start.59) | collective-permute-done | bytes 262176 | tf_op jit(solution)/shard_map/cond/branch_2_fun/ppermute | solution.py:55
  (41 shorter events, 13.7 us)
Async XLA Ops:
  1.6 12.7 %copy-start.19 = (bf16[1,256,256]{2,1,0:T(8,128)(2,1)S(1)}, bf16[1,256,256]{2,1,0:T(8,128)(2,1)}, u32[]{:S(2)}) copy-start(bf16[1,256,256]{2,1,0:T(8,128)(2,1)} %get-tuple-element.167.value_ref) | copy-start | bytes 393220 | tf_op jit(solution)/shard_map/cond
  2.7 3.7 %collective-permute-start.40 = (bf16[256,512]{1,0:T(8,128)(2,1)S(1)}, bf16[256,512]{1,0:T(8,128)(2,1)S(1)}, u32[]{:S(2)}, u32[]{:S(2)}) collective-permute-start(bf16[256,512]{1,0:T(8,128)(2,1)S(1)} %get-tuple-element.156), channel_id=1, source_target_pairs={{0,4},{4,0},{8,12},{12,8},{16,20},{20,16},{24,28},{28,24},{1,5},{5... | collective-permute-start | bytes 786440 | tf_op jit(solution)/shard_map/cond/branch_2_fun/ppermute | solution.py:41
  6.4 14.3 %copy-start.2 = (f32[1,512,256]{2,1,0:T(8,128)S(1)}, f32[1,512,256]{2,1,0:T(8,128)}, u32[]{:S(2)}) copy-start(f32[1,512,256]{2,1,0:T(8,128)} %get-tuple-element.159.key_ref.kw) | copy-start | bytes 1572868 | tf_op jit(solution)/shard_map/cond
  6.4 14.3 %copy-start.6 = (f32[1,512,256]{2,1,0:T(8,128)S(1)}, f32[1,512,256]{2,1,0:T(8,128)}, u32[]{:S(2)}) copy-start(f32[1,512,256]{2,1,0:T(8,128)} %get-tuple-element.160.value_ref.vw) | copy-start | bytes 1572868 | tf_op jit(solution)/shard_map/cond
  6.4 18.7 %collective-permute-start.42 = (bf16[512,256]{1,0:T(8,128)(2,1)S(1)}, bf16[512,256]{1,0:T(8,128)(2,1)S(1)}, u32[]{:S(2)}, u32[]{:S(2)}) collective-permute-start(bf16[512,256]{1,0:T(8,128)(2,1)S(1)} %get-tuple-element.157.refs_0_.a0), channel_id=1, source_target_pairs={{0,3},{1,2},{2,1},{3,0},{4,7},{5,6},{6,5},{7,4},{8,11},{9,10},{10,... | collective-permute-start | bytes 786440 | tf_op jit(solution)/shard_map/cond/branch_2_fun/ppermute | solution.py:50
  14.2 14.3 %collective-permute-start.51 = (bf16[256,512]{1,0:T(8,128)(2,1)S(1)}, bf16[256,512]{1,0:T(8,128)(2,1)S(1)}, u32[]{:S(2)}, u32[]{:S(2)}) collective-permute-start(bf16[256,512]{1,0:T(8,128)(2,1)S(1)} %branch_2_fun.16.cot_own), channel_id=1, source_target_pairs={{0,4},{4,0},{8,12},{12,8},{16,20},{20,16},{24,28},{28,24},{1,5},{5... | collective-permute-start | bytes 786440 | tf_op jit(solution)/shard_map/cond/branch_2_fun/ppermute | solution.py:41
  16.8 14.4 %collective-permute-start.41 = (bf16[512,256]{1,0:T(8,128)(2,1)S(1)}, bf16[512,256]{1,0:T(8,128)(2,1)S(1)}, u32[]{:S(2)}, u32[]{:S(2)}) collective-permute-start(bf16[512,256]{1,0:T(8,128)(2,1)S(1)} %get-tuple-element.157.refs_0_.a0), channel_id=1, source_target_pairs={{0,1},{1,0},{2,3},{3,2},{4,5},{5,4},{6,7},{7,6},{8,9},{9,8},{10,11... | collective-permute-start | bytes 786440 | tf_op jit(solution)/shard_map/cond/branch_2_fun/ppermute | solution.py:50
  18.7 14.8 %collective-permute-start.45 = (bf16[512,256]{1,0:T(8,128)(2,1)S(1)}, bf16[512,256]{1,0:T(8,128)(2,1)S(1)}, u32[]{:S(2)}, u32[]{:S(2)}) collective-permute-start(bf16[512,256]{1,0:T(8,128)(2,1)S(1)} %get-tuple-element.158.refs_4_.a0), channel_id=1, source_target_pairs={{0,3},{1,2},{2,1},{3,0},{4,7},{5,6},{6,5},{7,4},{8,11},{9,10},{10,... | collective-permute-start | bytes 786440 | tf_op jit(solution)/shard_map/cond/branch_2_fun/ppermute | solution.py:50
  20.7 26.6 %collective-permute-start.47 = (bf16[512,512]{1,0:T(8,128)(2,1)S(1)}, bf16[512,512]{1,0:T(8,128)(2,1)S(1)}, u32[]{:S(2)}, u32[]{:S(2)}) collective-permute-start(bf16[512,512]{1,0:T(8,128)(2,1)S(1)} %branch_2_fun.13.refs_8_), channel_id=1, source_target_pairs={{0,24},{4,28},{8,0},{12,4},{16,8},{20,12},{24,16},{28,20},{1,25},{... | collective-permute-start | bytes 1572872 | tf_op jit(solution)/shard_map/cond/branch_2_fun/ppermute | solution.py:46
  25.2 13.0 %collective-permute-start.43 = (bf16[512,256]{1,0:T(8,128)(2,1)S(1)}, bf16[512,256]{1,0:T(8,128)(2,1)S(1)}, u32[]{:S(2)}, u32[]{:S(2)}) collective-permute-start(bf16[512,256]{1,0:T(8,128)(2,1)S(1)} %collective-permute-done.42.refs_3_.a3), channel_id=1, source_target_pairs={{0,1},{1,0},{2,3},{3,2},{4,5},{5,4},{6,7},{7,6},{8,9},{9,8},{10,11... | collective-permute-start | bytes 786440 | tf_op jit(solution)/shard_map/cond/branch_2_fun/ppermute | solution.py:50
  28.5 27.6 %collective-permute-start.48 = (bf16[512,512]{1,0:T(8,128)(2,1)S(1)}, bf16[512,512]{1,0:T(8,128)(2,1)S(1)}, u32[]{:S(2)}, u32[]{:S(2)}) collective-permute-start(bf16[512,512]{1,0:T(8,128)(2,1)S(1)} %branch_2_fun.13.refs_8_), channel_id=1, source_target_pairs={{0,16},{4,20},{8,24},{12,28},{16,0},{20,4},{24,8},{28,12},{1,17},{... | collective-permute-start | bytes 1572872 | tf_op jit(solution)/shard_map/cond/branch_2_fun/ppermute | solution.py:46
  31.2 27.4 %collective-permute-start.49 = (bf16[512,512]{1,0:T(8,128)(2,1)S(1)}, bf16[512,512]{1,0:T(8,128)(2,1)S(1)}, u32[]{:S(2)}, u32[]{:S(2)}) collective-permute-start(bf16[512,512]{1,0:T(8,128)(2,1)S(1)} %branch_2_fun.13.refs_8_), channel_id=1, source_target_pairs={{0,8},{4,12},{8,16},{12,20},{16,24},{20,28},{24,0},{28,4},{1,9},{5... | collective-permute-start | bytes 1572872 | tf_op jit(solution)/shard_map/cond/branch_2_fun/ppermute | solution.py:46
  33.5 9.3 %collective-permute-start.44 = (bf16[512,256]{1,0:T(8,128)(2,1)S(1)}, bf16[512,256]{1,0:T(8,128)(2,1)S(1)}, u32[]{:S(2)}, u32[]{:S(2)}) collective-permute-start(bf16[512,256]{1,0:T(8,128)(2,1)S(1)} %get-tuple-element.158.refs_4_.a0), channel_id=1, source_target_pairs={{0,1},{1,0},{2,3},{3,2},{4,5},{5,4},{6,7},{7,6},{8,9},{9,8},{10,11... | collective-permute-start | bytes 786440 | tf_op jit(solution)/shard_map/cond/branch_2_fun/ppermute | solution.py:50
  38.2 12.6 %collective-permute-start.46 = (bf16[512,256]{1,0:T(8,128)(2,1)S(1)}, bf16[512,256]{1,0:T(8,128)(2,1)S(1)}, u32[]{:S(2)}, u32[]{:S(2)}) collective-permute-start(bf16[512,256]{1,0:T(8,128)(2,1)S(1)} %collective-permute-done.45.refs_7_.a3), channel_id=1, source_target_pairs={{0,1},{1,0},{2,3},{3,2},{4,5},{5,4},{6,7},{7,6},{8,9},{9,8},{10,11... | collective-permute-start | bytes 786440 | tf_op jit(solution)/shard_map/cond/branch_2_fun/ppermute | solution.py:50
  42.8 21.1 %collective-permute-start.52 = (bf16[256,512]{1,0:T(8,128)(2,1)S(1)}, bf16[256,512]{1,0:T(8,128)(2,1)S(1)}, u32[]{:S(2)}, u32[]{:S(2)}) collective-permute-start(bf16[256,512]{1,0:T(8,128)(2,1)S(1)} %get-tuple-element.169), channel_id=1, source_target_pairs={{0,8},{4,12},{8,16},{12,20},{16,24},{20,28},{24,0},{28,4},{1,9},{5... | collective-permute-start | bytes 786440 | tf_op jit(solution)/shard_map/cond/branch_2_fun/ppermute | solution.py:46
  47.4 21.0 %collective-permute-start.53 = (bf16[256,512]{1,0:T(8,128)(2,1)S(1)}, bf16[256,512]{1,0:T(8,128)(2,1)S(1)}, u32[]{:S(2)}, u32[]{:S(2)}) collective-permute-start(bf16[256,512]{1,0:T(8,128)(2,1)S(1)} %get-tuple-element.170), channel_id=1, source_target_pairs={{0,16},{4,20},{8,24},{12,28},{16,0},{20,4},{24,8},{28,12},{1,17},{... | collective-permute-start | bytes 786440 | tf_op jit(solution)/shard_map/cond/branch_2_fun/ppermute | solution.py:46
  50.8 22.3 %collective-permute-start.54 = (bf16[256,512]{1,0:T(8,128)(2,1)S(1)}, bf16[256,512]{1,0:T(8,128)(2,1)S(1)}, u32[]{:S(2)}, u32[]{:S(2)}) collective-permute-start(bf16[256,512]{1,0:T(8,128)(2,1)S(1)} %get-tuple-element.171), channel_id=1, source_target_pairs={{0,24},{4,28},{8,0},{12,4},{16,8},{20,12},{24,16},{28,20},{1,25},{... | collective-permute-start | bytes 786440 | tf_op jit(solution)/shard_map/cond/branch_2_fun/ppermute | solution.py:46
  56.1 19.6 %collective-permute-start.56 = (bf16[256,512]{1,0:T(8,128)(2,1)S(1)}, bf16[256,512]{1,0:T(8,128)(2,1)S(1)}, u32[]{:S(2)}, u32[]{:S(2)}) collective-permute-start(bf16[256,512]{1,0:T(8,128)(2,1)S(1)} %get-tuple-element.178), channel_id=1, source_target_pairs={{0,8},{4,12},{8,16},{12,20},{16,24},{20,28},{24,0},{28,4},{1,9},{5... | collective-permute-start | bytes 786440 | tf_op jit(solution)/shard_map/cond/branch_2_fun/ppermute | solution.py:46
  58.7 19.7 %collective-permute-start.57 = (bf16[256,512]{1,0:T(8,128)(2,1)S(1)}, bf16[256,512]{1,0:T(8,128)(2,1)S(1)}, u32[]{:S(2)}, u32[]{:S(2)}) collective-permute-start(bf16[256,512]{1,0:T(8,128)(2,1)S(1)} %get-tuple-element.179), channel_id=1, source_target_pairs={{0,16},{4,20},{8,24},{12,28},{16,0},{20,4},{24,8},{28,12},{1,17},{... | collective-permute-start | bytes 786440 | tf_op jit(solution)/shard_map/cond/branch_2_fun/ppermute | solution.py:46
  63.8 9.3 %copy-start.14 = (f32[1,512,256]{2,1,0:T(8,128)S(1)}, f32[1,512,256]{2,1,0:T(8,128)}, u32[]{:S(2)}) copy-start(f32[1,512,256]{2,1,0:T(8,128)} %get-tuple-element.173.vm) | copy-start | bytes 1572868 | tf_op jit(solution)/shard_map/cond
  63.8 14.5 %collective-permute-start.58 = (bf16[256,512]{1,0:T(8,128)(2,1)S(1)}, bf16[256,512]{1,0:T(8,128)(2,1)S(1)}, u32[]{:S(2)}, u32[]{:S(2)}) collective-permute-start(bf16[256,512]{1,0:T(8,128)(2,1)S(1)} %get-tuple-element.180), channel_id=1, source_target_pairs={{0,24},{4,28},{8,0},{12,4},{16,8},{20,12},{24,16},{28,20},{1,25},{... | collective-permute-start | bytes 786440 | tf_op jit(solution)/shard_map/cond/branch_2_fun/ppermute | solution.py:46
  68.4 12.5 %collective-permute-start.50 = (bf16[256,512]{1,0:T(8,128)(2,1)S(1)}, bf16[256,512]{1,0:T(8,128)(2,1)S(1)}, u32[]{:S(2)}, u32[]{:S(2)}) collective-permute-start(bf16[256,512]{1,0:T(8,128)(2,1)S(1)} %get-tuple-element.162), channel_id=1, source_target_pairs={{0,4},{4,0},{8,12},{12,8},{16,20},{20,16},{24,28},{28,24},{1,5},{5... | collective-permute-start | bytes 786440 | tf_op jit(solution)/shard_map/cond/branch_2_fun/ppermute | solution.py:41
  73.4 15.9 %collective-permute-start.55 = (bf16[256,512]{1,0:T(8,128)(2,1)S(1)}, bf16[256,512]{1,0:T(8,128)(2,1)S(1)}, u32[]{:S(2)}, u32[]{:S(2)}) collective-permute-start(bf16[256,512]{1,0:T(8,128)(2,1)S(1)} %get-tuple-element.176), channel_id=1, source_target_pairs={{0,128},{32,160},{64,192},{96,224},{128,256},{160,288},{192,320},{... | collective-permute-start | bytes 786440 | tf_op jit(solution)/shard_map/cond/branch_2_fun/ppermute | solution.py:55
  78.5 23.9 %collective-permute-start.59 = (bf16[256,512]{1,0:T(8,128)(2,1)S(1)}, bf16[256,512]{1,0:T(8,128)(2,1)S(1)}, u32[]{:S(2)}, u32[]{:S(2)}) collective-permute-start(bf16[256,512]{1,0:T(8,128)(2,1)S(1)} %get-tuple-element.183), channel_id=1, source_target_pairs={{0,128},{32,160},{64,192},{96,224},{128,256},{160,288},{192,320},{... | collective-permute-start | bytes 786440 | tf_op jit(solution)/shard_map/cond/branch_2_fun/ppermute | solution.py:55
  (2 other events, 10.2 us)

commit v2 on v1

v2 whole, which is shorter than its diff:
```python
from functools import partial

import jax
import jax.numpy as jnp
from jax import lax
from jax.experimental import pallas as pl
from jax.experimental.pallas import tpu as pltpu
from jax.sharding import PartitionSpec as P

D = 4096
scale = D ** (-0.5)
momentum_decay = 0.9
chunks = 2
bf16 = jnp.bfloat16
f32 = jnp.float32

vmem = pl.BlockSpec(memory_space=pltpu.VMEM)
smem = pl.BlockSpec(memory_space=pltpu.SMEM)
anywhere = pl.BlockSpec(memory_space=pl.ANY)


def call(kernel, outs, *operands, scratch=(), scalars=0, late=(), flops=0):
    moved = sum(a.size * a.dtype.itemsize for a in operands)
    moved += sum(o.size * o.dtype.itemsize for o in outs)
    return pl.pallas_call(
        kernel,
        out_shape=outs,
        in_specs=[
            smem if i < scalars else anywhere if i in late else vmem for i in range(len(operands))
        ],
        out_specs=[vmem] * len(outs),
        scratch_shapes=list(scratch),
        compiler_params=pltpu.CompilerParams(vmem_limit_bytes=24 * 2**20),
        cost_estimate=pl.CostEstimate(flops=flops, bytes_accessed=moved, transcendentals=0),
    )(*operands)


def like(shape, dtype):
    return jax.ShapeDtypeStruct(shape, dtype)


def after(blocks, *others):
    count = len(blocks)
    late = range(count, count + len(others))
    outs = [like(block.shape, block.dtype) for block in blocks]
    return call(partial(pass_kernel, count), outs, *blocks, *others, late=late)


def across(block):
    return lax.ppermute(block, "fsdp", [(i, i ^ 1) for i in range(lax.axis_size("fsdp"))])


def around(block, mask):
    return lax.ppermute(block, "fsdp", [(i, i ^ (2 * mask)) for i in range(lax.axis_size("fsdp"))])


def swapped(block, mask):
    return lax.ppermute(block, "tp", [(i, i ^ mask) for i in range(lax.axis_size("tp"))])


def from_partner(block, distance):
    count = lax.axis_size("rep")
    return lax.ppermute(block, "rep", [(i, (i + distance) % count) for i in range(count)])


def split_kernel(core_ref, tokens_ref, key_ref, value_ref, own_ref, send_ref):
    half = own_ref.shape[1]
    width = key_ref.shape[2]
    core = core_ref[0]
    own_ref[...] = tokens_ref[0, :, pl.ds(pl.multiple_of(core * half, half), half)]
    send_ref[:, :half] = tokens_ref[0, :, pl.ds(pl.multiple_of((1 - core) * half, half), half)]
    send_ref[:, half : half + width] = key_ref[0]
    send_ref[:, half + width :] = value_ref[0]


def join_kernel(own_ref, arrived_ref, *part_refs):
    rows = own_ref.shape[0]
    for at, part in enumerate(part_refs):
        width = part.shape[1]
        part[:rows] = own_ref[:, at * width : (at + 1) * width]
        part[rows:] = arrived_ref[:, at * width : (at + 1) * width]


def beside_kernel(key_ref, value_ref, late_ref, out_ref):
    width = key_ref.shape[2]
    out_ref[:, :width] = key_ref[0].astype(bf16)
    out_ref[:, width:] = value_ref[0].astype(bf16)


def pass_kernel(count, *refs):
    for given, out in zip(refs[:count], refs[-count:]):
        out[...] = given[...]


def partial_kernel(at_ref, a0, a1, a2, a3, send, arrived, *refs):
    p0, p1, p2, p3, held = refs[-5:]
    tokens, features = send.shape
    cots = slice(features // 2, features)
    for j, a in enumerate((a0, a1, a2, a3)):
        held[j] = a[...]
    for k, p in enumerate((p0, p1, p2, p3)):
        j = at_ref[k]
        total = lax.dot_general(
            held[j, :tokens], send[:, cots], (((0,), (0,)), ((), ())), preferred_element_type=f32
        )
        total += lax.dot_general(
            held[j, tokens:], arrived[:, cots], (((0,), (0,)), ((), ())), preferred_element_type=f32
        )
        p[...] = (total * scale).astype(p.dtype)


def update_kernel(at, learn_ref, p0, r1, r3, r2, kw, vw, km, vm, *refs):
    velocity_ref, moved_ref, short_ref = refs[-3:]
    rows = p0.shape[0]
    width = kw.shape[2]
    part = pl.ds(at * rows, rows)
    learn = learn_ref[0]
    gradient = p0[...] + r1[...].astype(f32) + r2[...].astype(f32) + r3[...].astype(f32)
    for i, (w, m) in enumerate(((kw, km), (vw, vm))):
        cols = slice(i * width, (i + 1) * width)
        velocity = momentum_decay * m[0, part] + gradient[:, cols]
        moved = w[0, part] - learn * velocity
        velocity_ref[:, cols] = velocity
        moved_ref[:, cols] = moved
        short_ref[:, cols] = moved.astype(bf16)


def finish_kernel(*refs):
    outs = refs[-4:]
    width = outs[0].shape[2]
    for at in range(chunks):
        velocity, moved, other = refs[3 * at : 3 * at + 3]
        rows = velocity.shape[0]
        part = pl.ds(at * rows, rows)
        averaged = 0.5 * (moved[...] + other[...].astype(f32))
        outs[0][0, part] = averaged[:, :width]
        outs[1][0, part] = averaged[:, width:]
        outs[2][0, part] = velocity[:, :width]
        outs[3][0, part] = velocity[:, width:]


def project_kernel(at_ref, late_ref, *refs):
    acts, weights = refs[: 4 * chunks], refs[4 * chunks : 4 * chunks + 4]
    mine_ref, other_ref, held = refs[4 * chunks + 4 :]
    for i, a in enumerate(acts):
        held[i] = a[...]
    depth = held.shape[2]
    total = None
    for m, w in enumerate(weights):
        for at in range(chunks):
            term = jnp.dot(
                held[4 * at + at_ref[m]],
                w[at * depth : (at + 1) * depth],
                preferred_element_type=f32,
            )
            total = term if total is None else total + term
    rows = mine_ref.shape[0]
    mine_ref[...] = total[:rows]
    other_ref[...] = total[rows:].astype(bf16)


def project_end_kernel(mine_ref, other_ref, key_ref, value_ref):
    width = key_ref.shape[2]
    total = (mine_ref[...] + other_ref[...].astype(f32)) * scale
    key_ref[0] = total[:, :width].astype(bf16)
    value_ref[0] = total[:, width:].astype(bf16)


def step(tokens, kw, vw, km, vm, kc, vc, learn, core, order, distance):
    _, rows, features = tokens.shape
    _, depth, width = kw.shape
    half = features // 2
    both = 2 * width
    own, send = call(
        split_kernel,
        [like((rows, half), bf16), like((rows, half + both), bf16)],
        core, tokens, kc, vc,
        scalars=1,
    )
    arrived = across(send)
    weight = call(beside_kernel, [like((depth, both), bf16)], kw, vw, arrived, late=[2])[0]
    a0, b0 = call(
        join_kernel, [like((2 * rows, half // chunks), bf16)] * chunks, own, arrived
    )
    piece = depth // chunks

    def partials(a0, a1, a2, a3, *others):
        return call(
            partial_kernel,
            [like((piece, both), f32)] + [like((piece, both), bf16)] * 3,
            order, a0, a1, a2, a3, send, arrived, *others,
            scalars=1,
            late=range(7, 7 + len(others)),
            scratch=[pltpu.VMEM((4,) + a0.shape, bf16)],
            flops=2 * 4 * piece * both * 2 * rows,
        )

    def reduced(p1, p2, p3):
        parts = p1, p2, p3
        return [around(parts[m - 1], m) for m in (2, 1, 3)]

    def updated(at, late, parts):
        return call(
            partial(update_kernel, at),
            [like((piece, both), f32)] * 2 + [like((piece, both), bf16)],
            learn, *parts, kw, vw, km, vm, *late,
            scalars=1,
            late=range(9, 9 + len(late)),
        )

    a3, a1 = swapped(a0, 3), swapped(a0, 1)
    a2 = swapped(a3, 1)
    b3, b1 = swapped(b0, 3), swapped(after([b0], a3)[0], 1)
    swaps = [around(weight, m) for m in (3, 1, 2)]
    weights = weight, swaps[1], swaps[2], swaps[0]
    own_a, *parts_a = partials(a0, a1, a2, a3)
    b2 = swapped(after([b3], own_a, *swaps)[0], 1)
    velocity_a, moved_a, short_a = updated(0, (), (own_a, *reduced(*parts_a)))
    partner_a = from_partner(short_a, distance)
    own_b, *parts_b = partials(b0, b1, b2, b3)
    parts_b = after(parts_b, short_a)
    own_b = after([own_b], partner_a)[0]
    velocity_b, moved_b, short_b = updated(1, (), (own_b, *reduced(*parts_b)))
    partner_b = from_partner(short_b, distance)
    partner_b = after([partner_b])[0]
    kept = [velocity_a, moved_a, partner_a, velocity_b, moved_b, partner_b]
    mine, sent = call(
        project_kernel,
        [like((rows, both), f32), like((rows, both), bf16)],
        order, short_b, a0, a1, a2, a3, b0, b1, b2, b3, *weights,
        scalars=1,
        late=[1],
        scratch=[pltpu.VMEM((4 * chunks,) + a0.shape, bf16)],
    )
    keys_out, values_out = call(
        project_end_kernel, [like((1, rows, width), bf16)] * 2, mine, across(sent)
    )
    averaged_key, averaged_value, key_velocity, value_velocity = call(
        finish_kernel, [like((1, depth, width), f32)] * 4, *kept
    )
    return keys_out, values_out, averaged_key, averaged_value, key_velocity, value_velocity


def body(tokens, kw, vw, km, vm, kc, vc, step_number):
    replicas = lax.axis_size("rep")
    at_x, core = lax.axis_index("fsdp") // 2, lax.axis_index("fsdp") % 2
    at_z = lax.axis_index("tp")
    order = jnp.stack([at_x ^ at_z ^ m for m in range(4)]).astype(jnp.int32)
    learn = 0.5 * (step_number.astype(f32) + 1.0) / 1000.0
    branches = [partial(step, distance=2**power % replicas) for power in range(4)]
    return lax.switch(
        step_number[0] % 4,
        branches,
        tokens, kw, vw, km, vm, kc, vc, learn, core.reshape(1).astype(jnp.int32), order,
    )


def solution(mesh):
    spread = P("rep", "fsdp", "tp")
    return jax.shard_map(
        body,
        mesh=mesh,
        in_specs=(spread,) * 7 + (P(),),
        out_specs=(spread,) * 6,
        check_vma=False,
    )
```

time: 105 us -> 97.8 us (0.931)
  the two profiles are of different devices: /device:TPU:33 before, /device:TPU:24 now
where the time goes in v2:
time: 97.8 us; the launch traced here: 99 us
  starting transfers between devices  66.4 us (68%)
  waiting for transfers between devices  22.1 us (23%)
  Pallas kernels  8.69 us (9%)
  between operations  1.32 us (1%)
    ppermute x9, starting transfers between devices, around(): lax.ppermute(block, 'fsdp', [(i, i ^ 2 * mask) for i in range(lax.axis_si...  29.8 us
    ppermute x6, starting transfers between devices, swapped(): lax.ppermute(block, 'tp', [(i, i ^ mask) for i in range(lax.axis_size('tp...  23.2 us
    ppermute x2, starting transfers between devices, from_partner(): lax.ppermute(block, 'rep', [(i, (i + distance) % count) for i in range(co...  9.38 us
    pallas_call x15, Pallas kernels, call(): pl.pallas_call(kernel, out_shape=outs, in_specs=[smem if i < scalars else...  8.69 us
    ppermute x6, waiting for transfers between devices, swapped(): lax.ppermute(block, 'tp', [(i, i ^ mask) for i in range(lax.axis_size('tp...  7.56 us
    ppermute x9, waiting for transfers between devices, around(): lax.ppermute(block, 'fsdp', [(i, i ^ 2 * mask) for i in range(lax.axis_si...  6.38 us
    ppermute x2, waiting for transfers between devices, from_partner(): lax.ppermute(block, 'rep', [(i, (i + distance) % count) for i in range(co...  6.27 us
    ppermute x2, starting transfers between devices, across(): lax.ppermute(block, 'fsdp', [(i, i ^ 1) for i in range(lax.axis_size('fsd...  3.97 us
  transfers between devices with their start and end apart: 19, of which 7 were waited for; matrix products, arithmetic and copies ran while one was open for 0% of the time, Pallas kernels for 5%

profile of v2, /device:TPU:24, one launch (start us, length us, event | category | flops | bytes accessed | tf_op | source)
XLA Modules:
  0.0 99.0 jit_solution(17733122966593745193)
XLA Ops:
  1.4 97.6 %conditional.1 = (bf16[1,256,256]{2,1,0:T(8,128)(2,1)}, bf16[1,256,256]{2,1,0:T(8,128)(2,1)}, f32[1,512,256]{2,1,0:T(8,128)}, f32[1,512,256]{2,1,0:T(8,128)}, f3...) conditional(s32[]{:T(128)} %clamp.3, (s32[1]{0:T(128)}, ...), branch_computations={%region_0.1_spmd, %region_1.2_spmd, %region_2.3_spmd, %region_3.4_... | conditional | flops 1073741824 | bytes 71828432 | solution.py:251
  2.7 2.1 %collective-permute-start.38 = (bf16[256,1024]{1,0:T(8,128)(2,1)S(1)}, bf16[256,1024]{1,0:T(8,128)(2,1)S(1)}, u32[]{:S(2)}, u32[]{:S(2)}) collective-permute-start(bf16[256,1024]{1,0:T(8,128)(2,1)S(1)} %get-tuple-element.165.send), channel_id=1, source_target_pairs={{0,4},{4,0},{8,12},{12,8},{16,20},{20,16},{24,28},{28,24},{1,5},{5... | collective-permute-start | bytes 1572872 | tf_op jit(solution)/shard_map/cond/branch_2_fun/ppermute | solution.py:50
  6.6 7.9 %collective-permute-start.39 = (bf16[512,256]{1,0:T(8,128)(2,1)S(1)}, bf16[512,256]{1,0:T(8,128)(2,1)S(1)}, u32[]{:S(2)}, u32[]{:S(2)}) collective-permute-start(bf16[512,256]{1,0:T(8,128)(2,1)S(1)} %get-tuple-element.167.a0.refs_0_), channel_id=1, source_target_pairs={{0,3},{1,2},{2,1},{3,0},{4,7},{5,6},{6,5},{7,4},{8,11},{9,10},{10,... | collective-permute-start | bytes 786440 | tf_op jit(solution)/shard_map/cond/branch_2_fun/ppermute | solution.py:58
  14.5 1.9 %collective-permute-start.42 = (bf16[512,256]{1,0:T(8,128)(2,1)S(1)}, bf16[512,256]{1,0:T(8,128)(2,1)S(1)}, u32[]{:S(2)}, u32[]{:S(2)}) collective-permute-start(bf16[512,256]{1,0:T(8,128)(2,1)S(1)} %get-tuple-element.167.a0.refs_0_), channel_id=1, source_target_pairs={{0,1},{1,0},{2,3},{3,2},{4,5},{5,4},{6,7},{7,6},{8,9},{9,8},{10,11... | collective-permute-start | bytes 786440 | tf_op jit(solution)/shard_map/cond/branch_2_fun/ppermute | solution.py:58
  16.6 4.9 %collective-permute-start.46 = (bf16[512,512]{1,0:T(8,128)(2,1)S(1)}, bf16[512,512]{1,0:T(8,128)(2,1)S(1)}, u32[]{:S(2)}, u32[]{:S(2)}) collective-permute-start(bf16[512,512]{1,0:T(8,128)(2,1)S(1)} %branch_2_fun.19.refs_8_), channel_id=1, source_target_pairs={{0,16},{4,20},{8,24},{12,28},{16,0},{20,4},{24,8},{28,12},{1,17},{... | collective-permute-start | bytes 1572872 | tf_op jit(solution)/shard_map/cond/branch_2_fun/ppermute | solution.py:54
  21.5 2.5 %collective-permute-start.45 = (bf16[512,512]{1,0:T(8,128)(2,1)S(1)}, bf16[512,512]{1,0:T(8,128)(2,1)S(1)}, u32[]{:S(2)}, u32[]{:S(2)}) collective-permute-start(bf16[512,512]{1,0:T(8,128)(2,1)S(1)} %branch_2_fun.19.refs_8_), channel_id=1, source_target_pairs={{0,8},{4,12},{8,0},{12,4},{16,24},{20,28},{24,16},{28,20},{1,9},{5... | collective-permute-start | bytes 1572872 | tf_op jit(solution)/shard_map/cond/branch_2_fun/ppermute | solution.py:54
  24.0 2.5 %collective-permute-start.44 = (bf16[512,512]{1,0:T(8,128)(2,1)S(1)}, bf16[512,512]{1,0:T(8,128)(2,1)S(1)}, u32[]{:S(2)}, u32[]{:S(2)}) collective-permute-start(bf16[512,512]{1,0:T(8,128)(2,1)S(1)} %branch_2_fun.19.refs_8_), channel_id=1, source_target_pairs={{0,24},{4,28},{8,16},{12,20},{16,8},{20,12},{24,0},{28,4},{1,25},{... | collective-permute-start | bytes 1572872 | tf_op jit(solution)/shard_map/cond/branch_2_fun/ppermute | solution.py:54
  26.5 3.9 %collective-permute-start.43 = (bf16[512,256]{1,0:T(8,128)(2,1)S(1)}, bf16[512,256]{1,0:T(8,128)(2,1)S(1)}, u32[]{:S(2)}, u32[]{:S(2)}) collective-permute-start(bf16[512,256]{1,0:T(8,128)(2,1)S(1)} %collective-permute-done.39.refs_1_.a3.refs_3_), channel_id=1, source_target_pairs={{0,1},{1,0},{2,3},{3,2},{4,5},{5,4},{6,7},{7,6},{8,9},{9,8},{10,11... | collective-permute-start | bytes 786440 | tf_op jit(solution)/shard_map/cond/branch_2_fun/ppermute | solution.py:58
  30.4 1.9 %collective-permute-start.41 = (bf16[512,256]{1,0:T(8,128)(2,1)S(1)}, bf16[512,256]{1,0:T(8,128)(2,1)S(1)}, u32[]{:S(2)}, u32[]{:S(2)}) collective-permute-start(bf16[512,256]{1,0:T(8,128)(2,1)S(1)} %get-tuple-element.166.refs_0_.a0.refs_4_), channel_id=1, source_target_pairs={{0,3},{1,2},{2,1},{3,0},{4,7},{5,6},{6,5},{7,4},{8,11},{9,10},{10,... | collective-permute-start | bytes 786440 | tf_op jit(solution)/shard_map/cond/branch_2_fun/ppermute | solution.py:58
  32.4 4.8 %collective-permute-done.43.a2.refs_2_ = bf16[512,256]{1,0:T(8,128)(2,1)S(1)} collective-permute-done((bf16[512,256]{1,0:T(8,128)(2,1)S(1)}, bf16[512,256]{1,0:T(8,128)(2,1)S(1)}, u32[]{:S(2)}, u32[]{:S(2)}) %collective-permute-start.43) | collective-permute-done | bytes 262176 | tf_op jit(solution)/shard_map/cond/branch_2_fun/ppermute | solution.py:58
  38.5 5.0 %collective-permute-start.48 = (bf16[256,512]{1,0:T(8,128)(2,1)S(1)}, bf16[256,512]{1,0:T(8,128)(2,1)S(1)}, u32[]{:S(2)}, u32[]{:S(2)}) collective-permute-start(bf16[256,512]{1,0:T(8,128)(2,1)S(1)} %get-tuple-element.172), channel_id=1, source_target_pairs={{0,16},{4,20},{8,24},{12,28},{16,0},{20,4},{24,8},{28,12},{1,17},{... | collective-permute-start | bytes 786440 | tf_op jit(solution)/shard_map/cond/branch_2_fun/ppermute | solution.py:54
  43.6 2.5 %collective-permute-start.49 = (bf16[256,512]{1,0:T(8,128)(2,1)S(1)}, bf16[256,512]{1,0:T(8,128)(2,1)S(1)}, u32[]{:S(2)}, u32[]{:S(2)}) collective-permute-start(bf16[256,512]{1,0:T(8,128)(2,1)S(1)} %get-tuple-element.173), channel_id=1, source_target_pairs={{0,8},{4,12},{8,0},{12,4},{16,24},{20,28},{24,16},{28,20},{1,9},{5... | collective-permute-start | bytes 786440 | tf_op jit(solution)/shard_map/cond/branch_2_fun/ppermute | solution.py:54
  46.1 2.6 %collective-permute-start.50 = (bf16[256,512]{1,0:T(8,128)(2,1)S(1)}, bf16[256,512]{1,0:T(8,128)(2,1)S(1)}, u32[]{:S(2)}, u32[]{:S(2)}) collective-permute-start(bf16[256,512]{1,0:T(8,128)(2,1)S(1)} %get-tuple-element.174), channel_id=1, source_target_pairs={{0,24},{4,28},{8,16},{12,20},{16,8},{20,12},{24,0},{28,4},{1,25},{... | collective-permute-start | bytes 786440 | tf_op jit(solution)/shard_map/cond/branch_2_fun/ppermute | solution.py:54
  48.7 5.5 %collective-permute-start.40 = (bf16[512,256]{1,0:T(8,128)(2,1)S(1)}, bf16[512,256]{1,0:T(8,128)(2,1)S(1)}, u32[]{:S(2)}, u32[]{:S(2)}) collective-permute-start(bf16[512,256]{1,0:T(8,128)(2,1)S(1)} %branch_2_fun.17), channel_id=1, source_target_pairs={{0,1},{1,0},{2,3},{3,2},{4,5},{5,4},{6,7},{7,6},{8,9},{9,8},{10,11... | collective-permute-start | bytes 786440 | tf_op jit(solution)/shard_map/cond/branch_2_fun/ppermute | solution.py:58
  54.3 2.1 %collective-permute-start.47 = (bf16[512,256]{1,0:T(8,128)(2,1)S(1)}, bf16[512,256]{1,0:T(8,128)(2,1)S(1)}, u32[]{:S(2)}, u32[]{:S(2)}) collective-permute-start(bf16[512,256]{1,0:T(8,128)(2,1)S(1)} %branch_2_fun.20), channel_id=1, source_target_pairs={{0,1},{1,0},{2,3},{3,2},{4,5},{5,4},{6,7},{7,6},{8,9},{9,8},{10,11... | collective-permute-start | bytes 786440 | tf_op jit(solution)/shard_map/cond/branch_2_fun/ppermute | solution.py:58
  56.6 4.8 %collective-permute-start.51 = (bf16[256,512]{1,0:T(8,128)(2,1)S(1)}, bf16[256,512]{1,0:T(8,128)(2,1)S(1)}, u32[]{:S(2)}, u32[]{:S(2)}) collective-permute-start(bf16[256,512]{1,0:T(8,128)(2,1)S(1)} %get-tuple-element.177.refs_3_), channel_id=1, source_target_pairs={{0,128},{32,160},{64,192},{96,224},{128,256},{160,288},{192,320},{... | collective-permute-start | bytes 786440 | tf_op jit(solution)/shard_map/cond/branch_2_fun/ppermute | solution.py:63
  61.4 2.7 %collective-permute-done.47.a2.refs_6_ = bf16[512,256]{1,0:T(8,128)(2,1)S(1)} collective-permute-done((bf16[512,256]{1,0:T(8,128)(2,1)S(1)}, bf16[512,256]{1,0:T(8,128)(2,1)S(1)}, u32[]{:S(2)}, u32[]{:S(2)}) %collective-permute-start.47) | collective-permute-done | bytes 262176 | tf_op jit(solution)/shard_map/cond/branch_2_fun/ppermute | solution.py:58
  65.6 3.2 %collective-permute-start.52 = (bf16[256,512]{1,0:T(8,128)(2,1)S(1)}, bf16[256,512]{1,0:T(8,128)(2,1)S(1)}, u32[]{:S(2)}, u32[]{:S(2)}) collective-permute-start(bf16[256,512]{1,0:T(8,128)(2,1)S(1)} %get-tuple-element.181), channel_id=1, source_target_pairs={{0,16},{4,20},{8,24},{12,28},{16,0},{20,4},{24,8},{28,12},{1,17},{... | collective-permute-start | bytes 786440 | tf_op jit(solution)/shard_map/cond/branch_2_fun/ppermute | solution.py:54
  68.8 2.8 %collective-permute-start.53 = (bf16[256,512]{1,0:T(8,128)(2,1)S(1)}, bf16[256,512]{1,0:T(8,128)(2,1)S(1)}, u32[]{:S(2)}, u32[]{:S(2)}) collective-permute-start(bf16[256,512]{1,0:T(8,128)(2,1)S(1)} %get-tuple-element.182), channel_id=1, source_target_pairs={{0,8},{4,12},{8,0},{12,4},{16,24},{20,28},{24,16},{28,20},{1,9},{5... | collective-permute-start | bytes 786440 | tf_op jit(solution)/shard_map/cond/branch_2_fun/ppermute | solution.py:54
  71.6 3.8 %collective-permute-start.54 = (bf16[256,512]{1,0:T(8,128)(2,1)S(1)}, bf16[256,512]{1,0:T(8,128)(2,1)S(1)}, u32[]{:S(2)}, u32[]{:S(2)}) collective-permute-start(bf16[256,512]{1,0:T(8,128)(2,1)S(1)} %get-tuple-element.183), channel_id=1, source_target_pairs={{0,24},{4,28},{8,16},{12,20},{16,8},{20,12},{24,0},{28,4},{1,25},{... | collective-permute-start | bytes 786440 | tf_op jit(solution)/shard_map/cond/branch_2_fun/ppermute | solution.py:54
  75.5 2.1 %collective-permute-done.52.r1 = bf16[256,512]{1,0:T(8,128)(2,1)S(1)} collective-permute-done((bf16[256,512]{1,0:T(8,128)(2,1)S(1)}, bf16[256,512]{1,0:T(8,128)(2,1)S(1)}, u32[]{:S(2)}, u32[]{:S(2)}) %collective-permute-start.52) | collective-permute-done | bytes 262176 | tf_op jit(solution)/shard_map/cond/branch_2_fun/ppermute | solution.py:54
  79.4 2.5 %collective-permute-done.54.r2 = bf16[256,512]{1,0:T(8,128)(2,1)S(1)} collective-permute-done((bf16[256,512]{1,0:T(8,128)(2,1)S(1)}, bf16[256,512]{1,0:T(8,128)(2,1)S(1)}, u32[]{:S(2)}, u32[]{:S(2)}) %collective-permute-start.54) | collective-permute-done | bytes 262176 | tf_op jit(solution)/shard_map/cond/branch_2_fun/ppermute | solution.py:54
  82.0 4.6 %collective-permute-start.56 = (bf16[256,512]{1,0:T(8,128)(2,1)S(1)}, bf16[256,512]{1,0:T(8,128)(2,1)S(1)}, u32[]{:S(2)}, u32[]{:S(2)}) collective-permute-start(bf16[256,512]{1,0:T(8,128)(2,1)S(1)} %get-tuple-element.184.late_ref), channel_id=1, source_target_pairs={{0,128},{32,160},{64,192},{96,224},{128,256},{160,288},{192,320},{... | collective-permute-start | bytes 786440 | tf_op jit(solution)/shard_map/cond/branch_2_fun/ppermute | solution.py:63
  90.5 6.3 %collective-permute-done.56.refs_0_ = bf16[256,512]{1,0:T(8,128)(2,1)S(1)} collective-permute-done((bf16[256,512]{1,0:T(8,128)(2,1)S(1)}, bf16[256,512]{1,0:T(8,128)(2,1)S(1)}, u32[]{:S(2)}, u32[]{:S(2)}) %collective-permute-start.56) | collective-permute-done | bytes 262176 | tf_op jit(solution)/shard_map/cond/branch_2_fun/ppermute | solution.py:63
  (39 shorter events, 14.4 us)
Async XLA Ops:
  1.4 15.1 %copy-start.6 = (f32[1,512,256]{2,1,0:T(8,128)S(1)}, f32[1,512,256]{2,1,0:T(8,128)}, u32[]{:S(2)}) copy-start(f32[1,512,256]{2,1,0:T(8,128)} %get-tuple-element.170.value_ref.vw) | copy-start | bytes 1572868 | tf_op jit(solution)/shard_map/cond
  2.6 13.8 %copy-start.2 = (f32[1,512,256]{2,1,0:T(8,128)S(1)}, f32[1,512,256]{2,1,0:T(8,128)}, u32[]{:S(2)}) copy-start(f32[1,512,256]{2,1,0:T(8,128)} %get-tuple-element.169.key_ref.kw) | copy-start | bytes 1572868 | tf_op jit(solution)/shard_map/cond
  2.7 3.9 %collective-permute-start.38 = (bf16[256,1024]{1,0:T(8,128)(2,1)S(1)}, bf16[256,1024]{1,0:T(8,128)(2,1)S(1)}, u32[]{:S(2)}, u32[]{:S(2)}) collective-permute-start(bf16[256,1024]{1,0:T(8,128)(2,1)S(1)} %get-tuple-element.165.send), channel_id=1, source_target_pairs={{0,4},{4,0},{8,12},{12,8},{16,20},{20,16},{24,28},{28,24},{1,5},{5... | collective-permute-start | bytes 1572872 | tf_op jit(solution)/shard_map/cond/branch_2_fun/ppermute | solution.py:50
  6.6 19.8 %collective-permute-start.39 = (bf16[512,256]{1,0:T(8,128)(2,1)S(1)}, bf16[512,256]{1,0:T(8,128)(2,1)S(1)}, u32[]{:S(2)}, u32[]{:S(2)}) collective-permute-start(bf16[512,256]{1,0:T(8,128)(2,1)S(1)} %get-tuple-element.167.a0.refs_0_), channel_id=1, source_target_pairs={{0,3},{1,2},{2,1},{3,0},{4,7},{5,6},{6,5},{7,4},{8,11},{9,10},{10,... | collective-permute-start | bytes 786440 | tf_op jit(solution)/shard_map/cond/branch_2_fun/ppermute | solution.py:58
  14.5 15.9 %collective-permute-start.42 = (bf16[512,256]{1,0:T(8,128)(2,1)S(1)}, bf16[512,256]{1,0:T(8,128)(2,1)S(1)}, u32[]{:S(2)}, u32[]{:S(2)}) collective-permute-start(bf16[512,256]{1,0:T(8,128)(2,1)S(1)} %get-tuple-element.167.a0.refs_0_), channel_id=1, source_target_pairs={{0,1},{1,0},{2,3},{3,2},{4,5},{5,4},{6,7},{7,6},{8,9},{9,8},{10,11... | collective-permute-start | bytes 786440 | tf_op jit(solution)/shard_map/cond/branch_2_fun/ppermute | solution.py:58
  16.6 29.5 %collective-permute-start.46 = (bf16[512,512]{1,0:T(8,128)(2,1)S(1)}, bf16[512,512]{1,0:T(8,128)(2,1)S(1)}, u32[]{:S(2)}, u32[]{:S(2)}) collective-permute-start(bf16[512,512]{1,0:T(8,128)(2,1)S(1)} %branch_2_fun.19.refs_8_), channel_id=1, source_target_pairs={{0,16},{4,20},{8,24},{12,28},{16,0},{20,4},{24,8},{28,12},{1,17},{... | collective-permute-start | bytes 1572872 | tf_op jit(solution)/shard_map/cond/branch_2_fun/ppermute | solution.py:54
  21.5 27.2 %collective-permute-start.45 = (bf16[512,512]{1,0:T(8,128)(2,1)S(1)}, bf16[512,512]{1,0:T(8,128)(2,1)S(1)}, u32[]{:S(2)}, u32[]{:S(2)}) collective-permute-start(bf16[512,512]{1,0:T(8,128)(2,1)S(1)} %branch_2_fun.19.refs_8_), channel_id=1, source_target_pairs={{0,8},{4,12},{8,0},{12,4},{16,24},{20,28},{24,16},{28,20},{1,9},{5... | collective-permute-start | bytes 1572872 | tf_op jit(solution)/shard_map/cond/branch_2_fun/ppermute | solution.py:54
  24.0 30.2 %collective-permute-start.44 = (bf16[512,512]{1,0:T(8,128)(2,1)S(1)}, bf16[512,512]{1,0:T(8,128)(2,1)S(1)}, u32[]{:S(2)}, u32[]{:S(2)}) collective-permute-start(bf16[512,512]{1,0:T(8,128)(2,1)S(1)} %branch_2_fun.19.refs_8_), channel_id=1, source_target_pairs={{0,24},{4,28},{8,16},{12,20},{16,8},{20,12},{24,0},{28,4},{1,25},{... | collective-permute-start | bytes 1572872 | tf_op jit(solution)/shard_map/cond/branch_2_fun/ppermute | solution.py:54
  26.5 10.7 %collective-permute-start.43 = (bf16[512,256]{1,0:T(8,128)(2,1)S(1)}, bf16[512,256]{1,0:T(8,128)(2,1)S(1)}, u32[]{:S(2)}, u32[]{:S(2)}) collective-permute-start(bf16[512,256]{1,0:T(8,128)(2,1)S(1)} %collective-permute-done.39.refs_1_.a3.refs_3_), channel_id=1, source_target_pairs={{0,1},{1,0},{2,3},{3,2},{4,5},{5,4},{6,7},{7,6},{8,9},{9,8},{10,11... | collective-permute-start | bytes 786440 | tf_op jit(solution)/shard_map/cond/branch_2_fun/ppermute | solution.py:58
  30.4 13.1 %collective-permute-start.41 = (bf16[512,256]{1,0:T(8,128)(2,1)S(1)}, bf16[512,256]{1,0:T(8,128)(2,1)S(1)}, u32[]{:S(2)}, u32[]{:S(2)}) collective-permute-start(bf16[512,256]{1,0:T(8,128)(2,1)S(1)} %get-tuple-element.166.refs_0_.a0.refs_4_), channel_id=1, source_target_pairs={{0,3},{1,2},{2,1},{3,0},{4,7},{5,6},{6,5},{7,4},{8,11},{9,10},{10,... | collective-permute-start | bytes 786440 | tf_op jit(solution)/shard_map/cond/branch_2_fun/ppermute | solution.py:58
  38.5 17.8 %collective-permute-start.48 = (bf16[256,512]{1,0:T(8,128)(2,1)S(1)}, bf16[256,512]{1,0:T(8,128)(2,1)S(1)}, u32[]{:S(2)}, u32[]{:S(2)}) collective-permute-start(bf16[256,512]{1,0:T(8,128)(2,1)S(1)} %get-tuple-element.172), channel_id=1, source_target_pairs={{0,16},{4,20},{8,24},{12,28},{16,0},{20,4},{24,8},{28,12},{1,17},{... | collective-permute-start | bytes 786440 | tf_op jit(solution)/shard_map/cond/branch_2_fun/ppermute | solution.py:54
  43.6 12.8 %collective-permute-start.49 = (bf16[256,512]{1,0:T(8,128)(2,1)S(1)}, bf16[256,512]{1,0:T(8,128)(2,1)S(1)}, u32[]{:S(2)}, u32[]{:S(2)}) collective-permute-start(bf16[256,512]{1,0:T(8,128)(2,1)S(1)} %get-tuple-element.173), channel_id=1, source_target_pairs={{0,8},{4,12},{8,0},{12,4},{16,24},{20,28},{24,16},{28,20},{1,9},{5... | collective-permute-start | bytes 786440 | tf_op jit(solution)/shard_map/cond/branch_2_fun/ppermute | solution.py:54
  46.1 10.3 %collective-permute-start.50 = (bf16[256,512]{1,0:T(8,128)(2,1)S(1)}, bf16[256,512]{1,0:T(8,128)(2,1)S(1)}, u32[]{:S(2)}, u32[]{:S(2)}) collective-permute-start(bf16[256,512]{1,0:T(8,128)(2,1)S(1)} %get-tuple-element.174), channel_id=1, source_target_pairs={{0,24},{4,28},{8,16},{12,20},{16,8},{20,12},{24,0},{28,4},{1,25},{... | collective-permute-start | bytes 786440 | tf_op jit(solution)/shard_map/cond/branch_2_fun/ppermute | solution.py:54
  48.7 12.7 %collective-permute-start.40 = (bf16[512,256]{1,0:T(8,128)(2,1)S(1)}, bf16[512,256]{1,0:T(8,128)(2,1)S(1)}, u32[]{:S(2)}, u32[]{:S(2)}) collective-permute-start(bf16[512,256]{1,0:T(8,128)(2,1)S(1)} %branch_2_fun.17), channel_id=1, source_target_pairs={{0,1},{1,0},{2,3},{3,2},{4,5},{5,4},{6,7},{7,6},{8,9},{9,8},{10,11... | collective-permute-start | bytes 786440 | tf_op jit(solution)/shard_map/cond/branch_2_fun/ppermute | solution.py:58
  54.2 2.1 %copy-start.10 = (f32[1,512,256]{2,1,0:T(8,128)S(1)}, f32[1,512,256]{2,1,0:T(8,128)}, u32[]{:S(2)}) copy-start(f32[1,512,256]{2,1,0:T(8,128)} %get-tuple-element.175.km) | copy-start | bytes 1572868 | tf_op jit(solution)/shard_map/cond
  54.2 2.1 %copy-start.14 = (f32[1,512,256]{2,1,0:T(8,128)S(1)}, f32[1,512,256]{2,1,0:T(8,128)}, u32[]{:S(2)}) copy-start(f32[1,512,256]{2,1,0:T(8,128)} %get-tuple-element.176.vm) | copy-start | bytes 1572868 | tf_op jit(solution)/shard_map/cond
  54.3 9.9 %collective-permute-start.47 = (bf16[512,256]{1,0:T(8,128)(2,1)S(1)}, bf16[512,256]{1,0:T(8,128)(2,1)S(1)}, u32[]{:S(2)}, u32[]{:S(2)}) collective-permute-start(bf16[512,256]{1,0:T(8,128)(2,1)S(1)} %branch_2_fun.20), channel_id=1, source_target_pairs={{0,1},{1,0},{2,3},{3,2},{4,5},{5,4},{6,7},{7,6},{8,9},{9,8},{10,11... | collective-permute-start | bytes 786440 | tf_op jit(solution)/shard_map/cond/branch_2_fun/ppermute | solution.py:58
  56.6 18.8 %collective-permute-start.51 = (bf16[256,512]{1,0:T(8,128)(2,1)S(1)}, bf16[256,512]{1,0:T(8,128)(2,1)S(1)}, u32[]{:S(2)}, u32[]{:S(2)}) collective-permute-start(bf16[256,512]{1,0:T(8,128)(2,1)S(1)} %get-tuple-element.177.refs_3_), channel_id=1, source_target_pairs={{0,128},{32,160},{64,192},{96,224},{128,256},{160,288},{192,320},{... | collective-permute-start | bytes 786440 | tf_op jit(solution)/shard_map/cond/branch_2_fun/ppermute | solution.py:63
  65.6 12.0 %collective-permute-start.52 = (bf16[256,512]{1,0:T(8,128)(2,1)S(1)}, bf16[256,512]{1,0:T(8,128)(2,1)S(1)}, u32[]{:S(2)}, u32[]{:S(2)}) collective-permute-start(bf16[256,512]{1,0:T(8,128)(2,1)S(1)} %get-tuple-element.181), channel_id=1, source_target_pairs={{0,16},{4,20},{8,24},{12,28},{16,0},{20,4},{24,8},{28,12},{1,17},{... | collective-permute-start | bytes 786440 | tf_op jit(solution)/shard_map/cond/branch_2_fun/ppermute | solution.py:54
  68.8 10.6 %collective-permute-start.53 = (bf16[256,512]{1,0:T(8,128)(2,1)S(1)}, bf16[256,512]{1,0:T(8,128)(2,1)S(1)}, u32[]{:S(2)}, u32[]{:S(2)}) collective-permute-start(bf16[256,512]{1,0:T(8,128)(2,1)S(1)} %get-tuple-element.182), channel_id=1, source_target_pairs={{0,8},{4,12},{8,0},{12,4},{16,24},{20,28},{24,16},{28,20},{1,9},{5... | collective-permute-start | bytes 786440 | tf_op jit(solution)/shard_map/cond/branch_2_fun/ppermute | solution.py:54
  71.6 10.3 %collective-permute-start.54 = (bf16[256,512]{1,0:T(8,128)(2,1)S(1)}, bf16[256,512]{1,0:T(8,128)(2,1)S(1)}, u32[]{:S(2)}, u32[]{:S(2)}) collective-permute-start(bf16[256,512]{1,0:T(8,128)(2,1)S(1)} %get-tuple-element.183), channel_id=1, source_target_pairs={{0,24},{4,28},{8,16},{12,20},{16,8},{20,12},{24,0},{28,4},{1,25},{... | collective-permute-start | bytes 786440 | tf_op jit(solution)/shard_map/cond/branch_2_fun/ppermute | solution.py:54
  82.0 14.7 %collective-permute-start.56 = (bf16[256,512]{1,0:T(8,128)(2,1)S(1)}, bf16[256,512]{1,0:T(8,128)(2,1)S(1)}, u32[]{:S(2)}, u32[]{:S(2)}) collective-permute-start(bf16[256,512]{1,0:T(8,128)(2,1)S(1)} %get-tuple-element.184.late_ref), channel_id=1, source_target_pairs={{0,128},{32,160},{64,192},{96,224},{128,256},{160,288},{192,320},{... | collective-permute-start | bytes 786440 | tf_op jit(solution)/shard_map/cond/branch_2_fun/ppermute | solution.py:63
  88.5 8.2 %collective-permute-start.55 = (bf16[256,512]{1,0:T(8,128)(2,1)S(1)}, bf16[256,512]{1,0:T(8,128)(2,1)S(1)}, u32[]{:S(2)}, u32[]{:S(2)}) collective-permute-start(bf16[256,512]{1,0:T(8,128)(2,1)S(1)} %get-tuple-element.186), channel_id=1, source_target_pairs={{0,4},{4,0},{8,12},{12,8},{16,20},{20,16},{24,28},{28,24},{1,5},{5... | collective-permute-start | bytes 786440 | tf_op jit(solution)/shard_map/cond/branch_2_fun/ppermute | solution.py:50
